TPU v7x, 32 devices: a whole 2x2x4 slice. The times are simulated.
32 devices in a mesh: group: 2 (over y), dp: 4 (over x, core), mp: 4 (over z).
Axes of the slice: x: 2, y: 2, z: 4, core: 2. Of those that a mesh axis runs over, the one named last changes fastest.
Arguments:
- tokens: bfloat16 [2048, 6144], P(('group', 'dp'), 'mp'), parts along dimension 0, may hold values from -40 to 40, as said below
- counts: int32 [8, 4, 2], P('group'), parts along dimension 0, may hold values from 1 to 48, 64 in all within a row
- ln_gain: float32 [6144], replicated, may hold values from 0.1 to 1.9
- w_qkv: bfloat16 [6144, 3, 3072], P('dp', None, 'mp'), may hold values from -0.078125 to 0.078125
- w_up: bfloat16 [6144, 12288], P('dp', 'mp'), may hold values from -0.078125 to 0.078125
- w_out: bfloat16 [3072, 6144], P('dp', 'mp'), may hold values from -0.109375 to 0.109375
- w_down: bfloat16 [12288, 6144], P('dp', 'mp'), may hold values from -0.0546875 to 0.0546875
Outputs:
- mixed: bfloat16 [2048, 6144], P(('group', 'dp'), 'mp'), parts along dimension 0
There are 2 independent parts, one for each index of `group`. A program takes and returns all parts, laid end to end along the dimension named above; an argument that names none is the same for every part. Nothing has to cross between parts.
Inputs may be any that keep to these rules, and one draw needn't show every extreme that they name: tokens have feature and row scales that differ. `counts`: each region of 64 rows is filled exactly by its 2 images.
All inputs are finite; a program needn't handle non-finite values.
Results may differ from a plain program's by a relative error of at most 0.0031.
Values may be sent and summed in bfloat16 or wider, within the bound.
A program may use at most 256 MiB of HBM per device.

v0:
```python
import jax
import jax.numpy as jnp
from jax import lax
from jax.sharding import PartitionSpec as P

HEADS = 24
HDIM = 128
IMGS = 2


def layer_norm(values, eps):
    mean = jnp.mean(values, axis=-1, keepdims=True)
    centred = values - mean
    variance = jnp.mean(centred * centred, axis=-1, keepdims=True)
    return centred * lax.rsqrt(variance + eps)


def attend(query_raw, query_ident, key_raw, key_ident, values):
    query_n = layer_norm(
        query_raw.reshape(query_raw.shape[0], HEADS, HDIM).astype(jnp.float32), 1e-06
    ).astype(jnp.bfloat16)
    key_n = layer_norm(
        key_raw.reshape(key_raw.shape[0], HEADS, HDIM).astype(jnp.float32), 1e-06
    ).astype(jnp.bfloat16)
    value_heads = values.reshape(values.shape[0], HEADS, HDIM)
    scores = jnp.einsum("qhd,khd->hqk", query_n, key_n, preferred_element_type=jnp.float32) * (
        1.0 / HDIM**0.5
    )
    same = (query_ident[:, None] == key_ident[None, :]).astype(jnp.float32)
    probs = jnp.exp(scores) * same[None]
    weights = (probs / jnp.sum(probs, axis=-1, keepdims=True)).astype(jnp.bfloat16)
    result = jnp.einsum(
        "hqk,khd->qhd", weights, value_heads, preferred_element_type=jnp.float32
    ).astype(jnp.bfloat16)
    return result.reshape(query_raw.shape[0], HEADS * HDIM)


def shards(tokens, counts, ln_gain, w_qkv, w_up, w_out, w_down):
    moved = lax.all_to_all(tokens, "dp", split_axis=0, concat_axis=0, tiled=True)
    full_qkv, full_up, full_out, full_down = (
        lax.all_gather(w_qkv, "dp", axis=0, tiled=True),
        lax.all_gather(w_up, "dp", axis=0, tiled=True),
        lax.all_gather(w_out, "dp", axis=0, tiled=True),
        lax.all_gather(w_down, "dp", axis=0, tiled=True),
    )
    whole = lax.all_gather(moved, "mp", axis=1, tiled=True)
    seq_rows = whole.shape[0]
    senders = counts.shape[0]
    region = seq_rows // senders
    receiver = lax.axis_index("dp")
    mine = lax.dynamic_index_in_dim(counts, receiver, axis=1, keepdims=False)
    bounds = jnp.cumsum(mine, axis=-1)
    position = jnp.arange(region)
    segment = jnp.sum((position[None, :, None] >= bounds[:, None, :]).astype(jnp.int32), axis=-1)
    sender_index = jnp.arange(senders)[:, None]
    ident = (sender_index * IMGS + segment).reshape(seq_rows)
    normed = (layer_norm(whole.astype(jnp.float32), 1e-06) * ln_gain).astype(jnp.bfloat16)
    part_cols = full_qkv.shape[2]
    qkv_part = jnp.dot(
        normed,
        full_qkv.reshape(full_qkv.shape[0], 3 * part_cols),
        preferred_element_type=jnp.float32,
    )
    qkv_part = qkv_part.astype(jnp.bfloat16).reshape(seq_rows, 3, part_cols)
    hidden_part = jax.nn.gelu(
        jnp.dot(normed, full_up, preferred_element_type=jnp.float32), approximate=False
    ).astype(jnp.bfloat16)
    qkv_all, hidden_all = (
        lax.all_gather(qkv_part, "mp", axis=2, tiled=True),
        lax.all_gather(hidden_part, "mp", axis=1, tiled=True),
    )
    attended = attend(qkv_all[:, 0], ident, qkv_all[:, 1], ident, qkv_all[:, 2])
    mixed = moved.astype(jnp.float32)
    mixed = mixed + jnp.dot(attended, full_out, preferred_element_type=jnp.float32)
    mixed = mixed + jnp.dot(hidden_all, full_down, preferred_element_type=jnp.float32)
    return mixed.astype(jnp.bfloat16)


def solution(mesh):
    return jax.shard_map(
        shards,
        mesh=mesh,
        in_specs=(
            P(("group", "dp"), "mp"),
            P("group", None, None),
            P(),
            P("dp", None, "mp"),
            P("dp", "mp"),
            P("dp", "mp"),
            P("dp", "mp"),
        ),
        out_specs=P(("group", "dp"), "mp"),
        check_vma=False,
    )
```

profile of v0, /device:TPU:0, one launch (start us, length us, event | category | flops | bytes accessed | tf_op | source)
XLA Modules:
  0.0 1016.7 jit_solution(9221549034626039199)
XLA Ops:
  6.5 0.0 copy-start
  6.5 0.0 all-gather.8.cloned.1.call-start
  6.5 16.7 %all_to_all.12 = bf16[4,64,1536]{2,1,0:T(8,128)(2,1)} all-to-all(bf16[4,64,1536]{2,1,0:T(8,128)(2,1)} %bitcast.31), channel_id=1, replica_groups=mesh['group'=2,'dp'=4,'mp'=4] {'dp'}, dimensions={0} | all-to-all | bytes 1572864 | tf_op jit(solution)/shard_map/all_to_all | solution.py:39
  23.2 0.0 all-gather.8.cloned.1.call-update
  23.2 0.0 all-gather.10.cloned.1.call-start
  23.3 10.4 %copy.19 = bf16[1536,3,768]{0,2,1:T(8,128)(2,1)} copy(bf16[1536,3,768]{2,0,1:T(8,128)(2,1)} %param.10) | data formatting | bytes 14155776 | tf_op args[3]
  33.7 0.0 all-gather.10.cloned.1.call-update
  33.7 0.0 all-gather.16.cloned.1.call-start
  33.7 0.0 copy-start.3
  33.7 0.7 all-gather.16.cloned.1.call-update
  34.4 0.0 all-gather.12.cloned.1.call-start
  34.5 53.5 %all-gather.8.cloned.1.call-done = bf16[256,6144]{1,0:T(8,128)(2,1)} async-done(((bf16[256,1536]{1,0:T(8,128)(2,1)}), bf16[256,6144]{1,0:T(8,128)(2,1)}) %all-gather.8.cloned.1.call-update) | async-done | bytes 3145744 | tf_op jit(solution)/shard_map/all_gather | solution.py:46
  88.0 0.0 copy-start.1
  88.0 2.5 convert_reduce_fusion
  90.6 0.3 copy-done.1
  90.8 1.0 fusion.2
  91.8 168.7 %all-gather.10.cloned.1.call-done = bf16[6144,3,768]{0,2,1:T(8,128)(2,1)} async-done(((bf16[1536,3,768]{0,2,1:T(8,128)(2,1)}), bf16[6144,3,768]{0,2,1:T(8,128)(2,1)}) %all-gather.10.cloned.1.call-update) | async-done | bytes 28311568 | tf_op jit(solution)/shard_map/all_gather | solution.py:41
  260.5 0.0 copy-done.3
  260.5 16.5 %convolution_convert_fusion = bf16[256,2304]{1,0:T(8,128)(2,1)} fusion(bf16[6144,2304]{0,1:T(8,128)(2,1)} %bitcast.33, bf16[256,6144]{1,0:T(8,128)(2,1)S(1)} %copy-done.1, f32[6144]{0:T(1024)S(1)} %copy-done.3, f32[256]{0:T(256)S(1)} %add_rsqrt_fusion.2, f32[256]{0:T(256)S(1)} %broadcast_multiply_fusion.2), kind=kOutput, calls=%fused_computation.15 | convolution fusion | flops 7256211456 | bytes 32663552 | tf_op jit(solution)/shard_map/dot_general | solution.py:59
  277.0 2.6 copy.20
  279.7 0.0 all-gather.12.cloned.1.call-update
  279.7 0.0 all-gather.14.cloned.1.call-start
  279.7 0.5 all-gather.14.cloned.1.call-update
  280.3 0.0 all-gather.20.cloned.1.call-start
  280.3 0.5 all-gather.20.cloned.1.call-update
  280.9 0.2 all-gather.18.cloned.1.call-start
  281.1 208.2 %all-gather.16.cloned.1.call-done = bf16[6144,3072]{1,0:T(8,128)(2,1)} async-done(((bf16[1536,3072]{1,0:T(8,128)(2,1)}), bf16[6144,3072]{1,0:T(8,128)(2,1)}) %all-gather.16.cloned.1.call-update) | async-done | bytes 37748752 | tf_op jit(solution)/shard_map/all_gather | solution.py:42
  489.3 24.1 %fusion.16 = bf16[256,3072]{1,0:T(8,128)(2,1)} fusion(bf16[6144,3072]{1,0:T(8,128)(2,1)} %all-gather.16.cloned.1.call-done, bf16[256,6144]{1,0:T(8,128)(2,1)S(1)} %copy-done.1, f32[6144]{0:T(1024)S(1)} %copy-done.3, f32[256]{0:T(256)S(1)} %add_rsqrt_fusion.2, f32[256]{0:T(256)S(1)} %broadcast_multiply_fusion.2), kind=kOutput, calls=%fused_computation.26 | convolution fusion | flops 9722658816 | bytes 42493952 | tf_op jit(solution)/shard_map/dot_general | solution.py:66
  513.4 0.0 all-gather.18.cloned.1.call-update
  513.4 0.0 copy-done
  513.4 0.1 constant_dynamic-slice_fusion
  513.5 0.1 copy.23
  513.6 0.1 convert_reduce_fusion.3
  513.7 0.1 broadcast_add_fusion
  513.8 0.1 add.63
  513.9 0.1 compare_convert_fusion
  514.0 66.2 %all-gather.12.cloned.1.call-done = bf16[256,3,3072]{0,2,1:T(8,128)(2,1)} async-done(((bf16[256,3,768]{0,2,1:T(8,128)(2,1)}), bf16[256,3,3072]{0,2,1:T(8,128)(2,1)}) %all-gather.12.cloned.1.call-update) | async-done | bytes 4718608 | tf_op jit(solution)/shard_map/all_gather | solution.py:69
  580.2 2.7 fusion.40
  582.9 0.2 convert_reduce_fusion.2
  583.1 0.2 convert_reduce_fusion.1
  583.4 0.5 fusion.12
  583.8 0.5 fusion.10
  584.3 2.0 fusion.5
  586.4 0.0 copy-start.2
  586.4 1.6 fusion.26
  588.0 56.3 %all-gather.14.cloned.1.call-done = bf16[3072,1536]{1,0:T(8,128)(2,1)} async-done(((bf16[768,1536]{1,0:T(8,128)(2,1)}), bf16[3072,1536]{1,0:T(8,128)(2,1)}) %all-gather.14.cloned.1.call-update) | async-done | bytes 9437200 | tf_op jit(solution)/shard_map/all_gather | solution.py:43
  644.3 0.0 copy-done.2
  644.3 7.5 convolution_add_fusion.1
  651.8 221.2 %all-gather.20.cloned.1.call-done = bf16[12288,1536]{1,0:T(8,128)(2,1)} async-done(((bf16[3072,1536]{1,0:T(8,128)(2,1)}), bf16[12288,1536]{1,0:T(8,128)(2,1)}) %all-gather.20.cloned.1.call-update) | async-done | bytes 37748752 | tf_op jit(solution)/shard_map/all_gather | solution.py:44
  873.1 117.0 %all-gather.18.cloned.1.call-done = bf16[256,12288]{1,0:T(8,128)(2,1)} async-done(((bf16[256,3072]{1,0:T(8,128)(2,1)}), bf16[256,12288]{1,0:T(8,128)(2,1)}) %all-gather.18.cloned.1.call-update) | async-done | bytes 6291472 | tf_op jit(solution)/shard_map/all_gather | solution.py:70
  990.0 19.9 %fusion.25 = bf16[256,1536]{1,0:T(8,128)(2,1)} fusion(f32[256,1536]{1,0:T(8,128)} %convolution_add_fusion.1, bf16[256,12288]{1,0:T(8,128)(2,1)} %all-gather.18.cloned.1.call-done, bf16[12288,1536]{1,0:T(8,128)(2,1)} %all-gather.20.cloned.1.call-done), kind=kOutput, calls=%fused_computation.45 | convolution fusion | flops 9664462848 | bytes 46399488 | tf_op jit(solution)/shard_map/dot_general | solution.py:75
  (7 shorter events, 0.1 us)
Async XLA Ops:
  6.5 506.9 %copy-start = (s32[4,4,2]{1,2,0:T(2,128)S(1)}, s32[4,4,2]{1,2,0:T(2,128)}, u32[]{:S(2)}) copy-start(s32[4,4,2]{1,2,0:T(2,128)} %param.8) | copy-start | bytes 388
  6.5 81.5 %all-gather.8.cloned.1.call-start = ((), (), s32[]{:S(2)}) async-start(), calls=%async_computation.1 | async-start | bytes 3932160 | tf_op jit(solution)/shard_map/all_gather | solution.py:46
  23.2 237.3 %all-gather.10.cloned.1.call-start = ((), (), s32[]{:S(2)}) async-start(), calls=%async_computation.2 | async-start | bytes 35389440 | tf_op jit(solution)/shard_map/all_gather | solution.py:41
  33.7 455.6 %all-gather.16.cloned.1.call-start = ((), (), s32[]{:S(2)}) async-start(), calls=%async_computation.5 | async-start | bytes 47185920 | tf_op jit(solution)/shard_map/all_gather | solution.py:42
  33.7 226.8 %copy-start.3 = (f32[6144]{0:T(1024)S(1)}, f32[6144]{0:T(1024)}, u32[]{:S(2)}) copy-start(f32[6144]{0:T(1024)} %param.9) | copy-start | bytes 73732
  34.4 545.8 %all-gather.12.cloned.1.call-start = ((), (), s32[]{:S(2)}) async-start(), calls=%async_computation.3 | async-start | bytes 5898240 | tf_op jit(solution)/shard_map/all_gather | solution.py:69
  88.0 2.8 copy-start.1
  279.7 364.6 %all-gather.14.cloned.1.call-start = ((), (), s32[]{:S(2)}) async-start(), calls=%async_computation.4 | async-start | bytes 11796480 | tf_op jit(solution)/shard_map/all_gather | solution.py:43
  280.3 592.8 %all-gather.20.cloned.1.call-start = ((), (), s32[]{:S(2)}) async-start(), calls=%async_computation.7 | async-start | bytes 47185920 | tf_op jit(solution)/shard_map/all_gather | solution.py:44
  280.9 709.2 %all-gather.18.cloned.1.call-start = ((), (), s32[]{:S(2)}) async-start(), calls=%async_computation.6 | async-start | bytes 7864320 | tf_op jit(solution)/shard_map/all_gather | solution.py:70
  586.4 58.0 %copy-start.2 = (bf16[4,64,1536]{2,1,0:T(8,128)(2,1)S(1)}, bf16[4,64,1536]{2,1,0:T(8,128)(2,1)}, u32[]{:S(2)}) copy-start(bf16[4,64,1536]{2,1,0:T(8,128)(2,1)} %all_to_all.12) | copy-start | bytes 2359300
Sparse Core Ops, SparseCore 0:
  23.3 64.6 all-gather.7
  89.6 170.8 all-gather.9
  262.1 227.2 all-gather.15
  490.7 89.4 all-gather.11
  581.6 62.6 all-gather.13
  645.8 227.2 all-gather.19
  874.6 115.3 all-gather.17
where the time goes:
time: 1020 us
  waiting for transfers between devices  893 us (88%)
  matrix products  71.6 us (7%)
  blocking collectives  16.7 us (2%)
  local copies, waits for them, and re-layouts  16.2 us (2%)
  between operations  13.6 us (1%)
    all_gather x1, waiting for transfers between devices, shards(): lax.all_gather(w_down, 'dp', axis=0, tiled=True)  221 us
    all_gather x1, waiting for transfers between devices, shards(): lax.all_gather(w_up, 'dp', axis=0, tiled=True)  208 us
    all_gather x1, waiting for transfers between devices, shards(): lax.all_gather(w_qkv, 'dp', axis=0, tiled=True)  169 us
    all_gather x1, waiting for transfers between devices, shards(): lax.all_gather(hidden_part, 'mp', axis=1, tiled=True)  117 us
    all_gather x1, waiting for transfers between devices, shards(): lax.all_gather(qkv_part, 'mp', axis=2, tiled=True)  66.2 us
    all_gather x1, waiting for transfers between devices, shards(): lax.all_gather(w_out, 'dp', axis=0, tiled=True)  56.3 us
    all_gather x1, waiting for transfers between devices, shards(): whole = lax.all_gather(moved, 'mp', axis=1, tiled=True)  53.5 us
    dot_general x1, matrix products, shards(): jnp.dot(normed, full_up, preferred_element_type=jnp.float32)  24.1 us
  transfers between devices with their start and end apart: 7, of which 7 were waited for; matrix products, arithmetic and copies ran while one was open for 7% of the time, Pallas kernels for 0%

commit v1 on v0

v1 whole, which is shorter than its diff:
```python
import jax
import jax.numpy as jnp
from jax import lax
from jax.sharding import PartitionSpec as P

HDIM = 128
IMGS = 2


def layer_norm(values, eps):
    mean = jnp.mean(values, axis=-1, keepdims=True)
    centred = values - mean
    variance = jnp.mean(centred * centred, axis=-1, keepdims=True)
    return centred * lax.rsqrt(variance + eps)


def attend(qkv, same):
    senders, region, _, width = qkv.shape
    heads = width // HDIM
    query_raw, key_raw, values = (
        qkv[:, :, part].reshape(senders, region, heads, HDIM) for part in range(3)
    )
    query_n = layer_norm(query_raw.astype(jnp.float32), 1e-06).astype(jnp.bfloat16)
    key_n = layer_norm(key_raw.astype(jnp.float32), 1e-06).astype(jnp.bfloat16)
    scores = jnp.einsum(
        "sqhd,skhd->shqk", query_n, key_n, preferred_element_type=jnp.float32
    ) * (1.0 / HDIM**0.5)
    probs = jnp.exp(scores) * same[:, None]
    weights = (probs / jnp.sum(probs, axis=-1, keepdims=True)).astype(jnp.bfloat16)
    result = jnp.einsum(
        "shqk,skhd->sqhd", weights, values, preferred_element_type=jnp.float32
    ).astype(jnp.bfloat16)
    return result.reshape(senders * region, width)


def exchange(values, n_dp, step):
    return lax.ppermute(values, "dp", [(index, index ^ step) for index in range(n_dp)])


def pick(values, index, size):
    return lax.dynamic_slice_in_dim(values, index, size, axis=0)


def sum_scatter(partial, n_dp):
    me = lax.axis_index("dp")
    assert n_dp & (n_dp - 1) == 0
    rest = partial.reshape(partial.shape[0], *partial.shape[1:])
    step = 1
    while step < n_dp:
        bit = (me // step) % 2
        halves = rest.reshape(rest.shape[0] // 2, 2, *rest.shape[1:])
        keep = lax.dynamic_index_in_dim(halves, bit, axis=1, keepdims=False)
        send = lax.dynamic_index_in_dim(halves, 1 - bit, axis=1, keepdims=False)
        got = exchange(send.astype(jnp.bfloat16), n_dp, step)
        rest = keep.astype(jnp.float32) + got.astype(jnp.float32)
        step *= 2
    return rest[0]


def make(n_dp, n_mp):
    def shards(tokens, counts, ln_gain, w_qkv, w_up, w_out, w_down):
        rows, cols = tokens.shape
        depth, _, part_cols = w_qkv.shape
        senders = counts.shape[0]
        region = rows // senders
        me = lax.axis_index("dp")

        whole = lax.all_gather(tokens, "mp", axis=1, tiled=True)
        normed = (layer_norm(whole.astype(jnp.float32), 1e-06) * ln_gain).astype(jnp.bfloat16)
        fed = lax.all_to_all(normed, "dp", split_axis=1, concat_axis=0, tiled=True)
        fed = fed.reshape(senders, n_dp, region, depth).transpose(1, 0, 2, 3)
        fed = fed.reshape(n_dp * rows, depth)
        moved = lax.all_to_all(tokens, "dp", split_axis=0, concat_axis=0, tiled=True)

        qkv_sum = jnp.dot(
            fed, w_qkv.reshape(depth, 3 * part_cols), preferred_element_type=jnp.float32
        )
        qkv = sum_scatter(qkv_sum.reshape(n_dp, rows, 3 * part_cols), n_dp).astype(jnp.bfloat16)
        up_sum = jnp.dot(fed, w_up, preferred_element_type=jnp.float32)
        hidden = jax.nn.gelu(
            sum_scatter(up_sum.reshape(n_dp, rows, up_sum.shape[1]), n_dp), approximate=False
        ).astype(jnp.bfloat16)

        mine = lax.dynamic_index_in_dim(counts, me, axis=1, keepdims=False)
        bounds = jnp.cumsum(mine, axis=-1)
        position = jnp.arange(region)
        segment = jnp.sum((position[None, :, None] >= bounds[:, None, :]).astype(jnp.int32), axis=-1)
        same = (segment[:, :, None] == segment[:, None, :]).astype(jnp.float32)

        qkv = qkv.reshape(rows, 3, part_cols)
        if part_cols % HDIM:
            qkv = lax.all_gather(qkv, "mp", axis=2, tiled=True)
            attended = attend(qkv.reshape(senders, region, 3, qkv.shape[2]), same)
        else:
            attended = attend(qkv.reshape(senders, region, 3, part_cols), same)
            attended = lax.all_gather(attended, "mp", axis=1, tiled=True)
        hidden = lax.all_gather(hidden, "mp", axis=1, tiled=True)
        attended = lax.all_to_all(attended, "dp", split_axis=1, concat_axis=0, tiled=True)
        hidden = lax.all_to_all(hidden, "dp", split_axis=1, concat_axis=0, tiled=True)

        mixed = jnp.dot(attended, w_out, preferred_element_type=jnp.float32)
        mixed = mixed + jnp.dot(hidden, w_down, preferred_element_type=jnp.float32)
        mixed = sum_scatter(mixed.reshape(n_dp, rows, cols), n_dp)
        return (moved.astype(jnp.float32) + mixed).astype(jnp.bfloat16)

    return shards


def solution(mesh):
    return jax.shard_map(
        make(mesh.shape["dp"], mesh.shape["mp"]),
        mesh=mesh,
        in_specs=(
            P(("group", "dp"), "mp"),
            P("group", None, None),
            P(),
            P("dp", None, "mp"),
            P("dp", "mp"),
            P("dp", "mp"),
            P("dp", "mp"),
        ),
        out_specs=P(("group", "dp"), "mp"),
        check_vma=False,
    )
```

time: 1020 us -> 516 us (0.51)
  waiting for transfers between devices: 893 us -> 314 us
  other arithmetic: 5.26 us -> 44.2 us
  local copies, waits for them, and re-layouts: 16.2 us -> 53.6 us
  matrix products: 71.6 us -> 44.3 us
  starting transfers between devices: 0.42 us -> 17 us
  blocking collectives: 16.7 us -> 27.7 us
    all_gather x7 -> x3, waiting for transfers between devices: 891 us -> 198 us  [the longest x1 109 us: shards(): hidden = lax.all_gather(hidden, 'mp', axis=1, tiled=True)]
    all_to_all x0 -> x3, waiting for transfers between devices: none -> 91.4 us  [the longest x1 64.8 us: shards(): lax.all_to_all(hidden, 'dp', split_axis=1, concat_axis=0, tiled=True)]
    dot_general x6, matrix products: 71.6 us -> 44.3 us  [the longest x1 14.7 us: shards(): mixed = mixed + jnp.dot(hidden, w_down, preferred_element_type=jnp.float32)]
    ppermute x0 -> x6, waiting for transfers between devices: none -> 24.9 us  [exchange(): lax.ppermute(values, 'dp', [(index, index ^ step) for index in range(n_dp)])]
    convert_element_type x1 -> x7, other arithmetic: 0.1 us -> 23.3 us  [the longest x1 9.01 us: shards(): hidden = jax.nn.gelu(sum_scatter(up_sum.reshape(n_dp, rows, up_sum.shape[...]
    all_to_all x0 -> x3, starting transfers between devices: none -> 14.2 us  [the longest x1 5.24 us: shards(): lax.all_to_all(hidden, 'dp', split_axis=1, concat_axis=0, tiled=True)]
    all_to_all x0 -> x3, local copies, waits for them, and re-layouts: none -> 13.5 us  [the longest x1 6.03 us: shards(): lax.all_to_all(hidden, 'dp', split_axis=1, concat_axis=0, tiled=True)]
    unnamed x9 -> x23, local copies, waits for them, and re-layouts: 10.7 us -> 23.2 us
  transfers between devices with their start and end apart: 7 -> 12, of which waited for: 7 -> 9; matrix products, arithmetic and copies ran while one was open for 7% -> 17% of each run, Pallas kernels for 0% -> 0%
where the time goes in v1:
time: 516 us; the launch traced here: 515 us
  waiting for transfers between devices  314 us (61%)
  local copies, waits for them, and re-layouts  53.6 us (10%)
  matrix products  44.3 us (9%)
  other arithmetic  44.2 us (9%)
  blocking collectives  27.7 us (5%)
  starting transfers between devices  17 us (3%)
  between operations  13.4 us (3%)
    all_gather x1, waiting for transfers between devices, shards(): hidden = lax.all_gather(hidden, 'mp', axis=1, tiled=True)  109 us
    all_gather x1, waiting for transfers between devices, shards(): whole = lax.all_gather(tokens, 'mp', axis=1, tiled=True)  66.4 us
    all_to_all x1, waiting for transfers between devices, shards(): lax.all_to_all(hidden, 'dp', split_axis=1, concat_axis=0, tiled=True)  64.8 us
    all_to_all x1, blocking collectives, shards(): lax.all_to_all(tokens, 'dp', split_axis=0, concat_axis=0, tiled=True)  27.7 us
    all_to_all x1, waiting for transfers between devices, shards(): fed = lax.all_to_all(normed, 'dp', split_axis=1, concat_axis=0, tiled=True)  26.6 us
    ppermute x6, waiting for transfers between devices, exchange(): lax.ppermute(values, 'dp', [(index, index ^ step) for index in range(n_dp)])  24.9 us
    unnamed x23, local copies, waits for them, and re-layouts  23.2 us
    all_gather x1, waiting for transfers between devices, shards(): attended = lax.all_gather(attended, 'mp', axis=1, tiled=True)  22.9 us
  transfers between devices with their start and end apart: 12, of which 9 were waited for; matrix products, arithmetic and copies ran while one was open for 17% of the time, Pallas kernels for 0%

profile of v1, /device:TPU:0, one launch (start us, length us, event | category | flops | bytes accessed | tf_op | source)
XLA Modules:
  0.0 514.6 jit_solution(16778328086728119014)
XLA Ops:
  6.5 2.4 copy.40
  9.0 66.4 %all-gather.4.cloned.1.call-done = bf16[256,6144]{0,1:T(8,128)(2,1)} async-done(((bf16[256,1536]{0,1:T(8,128)(2,1)}), bf16[256,6144]{0,1:T(8,128)(2,1)}) %all-gather.4.cloned.1.call-update) | async-done | bytes 3145744 | tf_op jit(solution)/shard_map/all_gather | solution.py:68
  75.4 2.9 convert_reduce_fusion
  78.2 0.9 fusion.4
  79.1 2.4 fusion.6
  81.5 4.6 all-to-all-start.1
  86.2 10.3 %copy.43 = bf16[1536,3,768]{0,2,1:T(8,128)(2,1)} copy(bf16[1536,3,768]{2,0,1:T(8,128)(2,1)} %param.10) | data formatting | bytes 14155776 | tf_op args[3]
  96.5 26.6 %all-to-all-done.1 = bf16[256,4,1536]{0,2,1:T(8,128)(2,1)} async-done(((bf16[256,4,1536]{0,2,1:T(8,128)(2,1)}), bf16[256,4,1536]{0,2,1:T(8,128)(2,1)}, u32[]{:S(2)}, u32[]{:S(2)}) %all-to-all-start.1) | async-done | bytes 3145760 | tf_op jit(solution)/shard_map/all_to_all | solution.py:70
  123.1 4.7 copy.41
  127.8 2.1 copy.42
  129.9 9.6 %fusion.41 = f32[2,2,256,2304]{3,2,1,0:T(8,128)S(1)} fusion(bf16[2,2,256,1536]{3,2,1,0:T(8,128)(2,1)S(1)} %bitcast.145, bf16[1536,2304,1,1]{0,1,3,2:T(8,128)(2,1)} %bitcast.140), kind=kOutput, calls=%fused_computation.84 | convolution fusion | flops 7247757312 | bytes 19660800 | tf_op jit(solution)/shard_map/dot_general | solution.py:75
  139.6 1.8 fusion.26
  141.4 2.5 copy-done.5
  143.8 12.4 %fusion = f32[2,2,256,3072]{3,2,1,0:T(8,128)S(1)} fusion(bf16[2,2,256,1536]{3,2,1,0:T(8,128)(2,1)S(1)} %bitcast.146, bf16[1536,3072]{1,0:T(8,128)(2,1)} %param.11), kind=kOutput, calls=%fused_computation | convolution fusion | flops 9663676416 | bytes 25165824 | tf_op jit(solution)/shard_map/dot_general | solution.py:79
  156.3 4.6 copy-done.4
  160.8 2.2 fusion.10
  163.1 0.5 collective-permute-start.2
  163.6 0.1 copy.47
  163.9 0.7 compare_convert_fusion
  164.6 3.7 bitcast_add_fusion.1
  168.3 0.1 dynamic-slice_convert_fusion.3
  168.4 0.4 collective-permute-start.1
  168.9 0.3 collective-permute-done.2
  169.2 4.6 bitcast_add_fusion
  173.8 2.7 copy-done.2
  176.4 1.4 dynamic-slice_convert_fusion.2
  177.9 1.3 collective-permute-start.3
  179.2 18.1 %collective-permute-done.1 = bf16[1,256,2304]{2,1,0:T(8,128)(2,1)S(1)} collective-permute-done((bf16[1,256,2304]{2,1,0:T(8,128)(2,1)S(1)}, bf16[1,256,2304]{2,1,0:T(8,128)(2,1)S(1)}, u32[]{:S(2)}, u32[]{:S(2)}) %collective-permute-start.1) | collective-permute-done | bytes 1179680 | tf_op jit(solution)/shard_map/ppermute | solution.py:37
  197.3 0.2 add_convert_fusion
  197.6 1.9 convert_element_type.139
  199.5 7.3 %fusion.33 = (f32[4,64,768]{2,1,0:T(8,128)}, f32[4,64,768]{2,1,0:T(8,128)}) fusion(bf16[4,64,3,768]{3,2,1,0:T(4,128)(2,1)} %convert_element_type.139), kind=kLoop, calls=%fused_computation.64 | loop fusion | flops 393216 | bytes 2359296 | tf_op jit(solution)/shard_map/convert_element_type | solution.py:23
  206.8 1.3 reshape.120
  208.1 1.0 reduce_sum.74
  209.1 0.9 broadcast_multiply_fusion.1
  210.0 0.6 multiply_reduce_fusion.1
  210.6 0.7 add_rsqrt_fusion.1
  211.3 2.2 reshape.121
  213.5 2.2 reduce_sum.76
  215.7 0.9 broadcast_multiply_fusion
  216.7 1.9 multiply_reduce_fusion
  218.6 2.4 multiply_convert_fusion
  221.0 0.3 fusion.30
  221.4 3.1 slice_reduce_fusion
  224.5 1.3 fusion.31
  225.8 0.3 copy.50
  226.1 0.8 copy.76
  227.0 3.0 collective-permute-done.3
  230.0 9.0 %fusion.9 = bf16[256,3072]{1,0:T(8,128)(2,1)} fusion(bf16[1,256,3072]{2,1,0:T(8,128)(2,1)} %collective-permute-done.3, f32[2,256,3072]{2,1,0:T(8,128)} %copy-done.2, s32[]{:T(128)S(6)} %select_n.63), kind=kLoop, calls=%fused_computation.18 | loop fusion | flops 52690944 | bytes 6291460 | tf_op jit(solution)/shard_map/convert_element_type | solution.py:82
  239.0 22.9 %all-gather.6.cloned.1.call-done = bf16[256,3072]{1,0:T(8,128)(2,1)} async-done(((bf16[256,768]{1,0:T(8,128)(2,1)}), bf16[256,3072]{1,0:T(8,128)(2,1)}) %all-gather.6.cloned.1.call-update) | async-done | bytes 1572880 | tf_op jit(solution)/shard_map/all_gather | solution.py:96
  261.9 2.7 copy.75
  264.6 4.3 all-to-all-start.2
  269.0 108.8 %all-gather.8.cloned.1.call-done = bf16[256,12288]{1,0:T(8,128)(2,1)} async-done(((bf16[256,3072]{1,0:T(8,128)(2,1)}), bf16[256,12288]{1,0:T(8,128)(2,1)}) %all-gather.8.cloned.1.call-update) | async-done | bytes 6291472 | tf_op jit(solution)/shard_map/all_gather | solution.py:97
  377.8 6.0 %copy.74 = bf16[32,4,8,3072]{3,2,0,1:T(8,128)(2,1)} copy(bf16[32,4,8,3072]{3,2,1,0:T(8,128)(2,1)} %bitcast.141) | data formatting | bytes 12582912 | tf_op jit(solution)/shard_map/all_to_all | solution.py:99
  383.8 5.2 %all-to-all-start.3 = ((bf16[256,4,3072]{2,0,1:T(8,128)(2,1)}), bf16[256,4,3072]{2,0,1:T(8,128)(2,1)}, u32[]{:S(2)}, u32[]{:S(2)}) async-start(bf16[256,4,3072]{2,0,1:T(8,128)(2,1)} %bitcast.137), calls=%async_computation.3 | async-start | bytes 12582912 | tf_op jit(solution)/shard_map/all_to_all | solution.py:99
  389.1 5.9 %fusion.42 = f32[1024,1536]{1,0:T(8,128)} fusion(bf16[1024,768]{1,0:T(8,128)(2,1)} %bitcast.14, bf16[768,1536]{1,0:T(8,128)(2,1)S(1)} %copy-done), kind=kOutput, calls=%fused_computation.85 | convolution fusion | flops 2415919104 | bytes 10223616 | tf_op jit(solution)/shard_map/dot_general | solution.py:101
  395.0 64.8 %all-to-all-done.3 = bf16[256,4,3072]{2,0,1:T(8,128)(2,1)} async-done(((bf16[256,4,3072]{2,0,1:T(8,128)(2,1)}), bf16[256,4,3072]{2,0,1:T(8,128)(2,1)}, u32[]{:S(2)}, u32[]{:S(2)}) %all-to-all-start.3) | async-done | bytes 6291488 | tf_op jit(solution)/shard_map/all_to_all | solution.py:99
  459.7 14.7 %convolution_add_fusion = f32[1024,1536]{1,0:T(8,128)S(1)} fusion(f32[1024,1536]{1,0:T(8,128)} %fusion.42, bf16[1024,3072]{1,0:T(8,128)(2,1)} %bitcast.22, bf16[3072,1536]{1,0:T(8,128)(2,1)} %param.13), kind=kOutput, calls=%fused_computation.15 | convolution fusion | flops 9665249280 | bytes 28311552 | tf_op jit(solution)/shard_map/dot_general | solution.py:102
  474.4 0.2 fusion.27
  474.7 3.4 collective-permute-done.4
  478.1 0.5 bitcast_add_fusion.2
  478.6 0.1 dynamic-slice_convert_fusion.4
  478.7 0.4 collective-permute-start.5
  479.1 27.7 %all_to_all.63 = bf16[4,64,1536]{2,1,0:T(8,128)(2,1)S(1)} all-to-all(bf16[4,64,1536]{2,1,0:T(8,128)(2,1)S(1)} %bitcast.147), channel_id=1, replica_groups=mesh['group'=2,'dp'=4,'mp'=4] {'dp'}, dimensions={0} | all-to-all | bytes 1572864 | tf_op jit(solution)/shard_map/all_to_all | solution.py:73
  506.8 1.3 fusion.28
  (34 shorter events, 0.5 us)
Async XLA Ops:
  6.5 382.5 %copy-start = (bf16[768,1536]{1,0:T(8,128)(2,1)S(1)}, bf16[768,1536]{1,0:T(8,128)(2,1)}, u32[]{:S(2)}) copy-start(bf16[768,1536]{1,0:T(8,128)(2,1)} %param.12) | copy-start | bytes 7077892
  6.5 68.8 %all-gather.4.cloned.1.call-start = ((), (), s32[]{:S(2)}) async-start(), calls=%async_computation.4 | async-start | bytes 3932160 | tf_op jit(solution)/shard_map/all_gather | solution.py:68
  75.4 2.9 copy-start.1
  75.4 3.8 copy-start.8
  81.5 41.6 %all-to-all-start.1 = ((bf16[256,4,1536]{0,2,1:T(8,128)(2,1)}), bf16[256,4,1536]{0,2,1:T(8,128)(2,1)}, u32[]{:S(2)}, u32[]{:S(2)}) async-start(bf16[256,4,1536]{0,2,1:T(8,128)(2,1)} %bitcast.138), calls=%async_computation.1 | async-start | bytes 6291456 | tf_op jit(solution)/shard_map/all_to_all | solution.py:70
  86.1 175.8 %all-gather.6.cloned.1.call-start = ((), (), s32[]{:S(2)}) async-start(), calls=%async_computation.5 | async-start | bytes 1966080 | tf_op jit(solution)/shard_map/all_gather | solution.py:96
  139.6 4.3 copy-start.5
  143.8 20.8 %collective-permute-start = (bf16[2,256,2304]{2,1,0:T(8,128)(2,1)}, bf16[2,256,2304]{2,1,0:T(8,128)(2,1)}, u32[]{:S(2)}, u32[]{:S(2)}) collective-permute-start(bf16[2,256,2304]{2,1,0:T(8,128)(2,1)} %fusion.26), channel_id=1, source_target_pairs={{0,4},{4,0},{8,12},{12,8},{1,5},{5,1},{9,13},{13,9},{2,6},{6,2},{1... | collective-permute-start | bytes 7077896 | tf_op jit(solution)/shard_map/ppermute | solution.py:37
  156.3 4.6 copy-start.4
  160.8 2.7 copy-start.9
  163.1 6.1 %collective-permute-start.2 = (bf16[2,256,3072]{2,1,0:T(8,128)(2,1)}, bf16[2,256,3072]{2,1,0:T(8,128)(2,1)}, u32[]{:S(2)}, u32[]{:S(2)}) collective-permute-start(bf16[2,256,3072]{2,1,0:T(8,128)(2,1)} %fusion.10), channel_id=1, source_target_pairs={{0,4},{4,0},{8,12},{12,8},{1,5},{5,1},{9,13},{13,9},{2,6},{6,2},{1... | collective-permute-start | bytes 9437192 | tf_op jit(solution)/shard_map/ppermute | solution.py:37
  168.4 28.9 %collective-permute-start.1 = (bf16[1,256,2304]{2,1,0:T(8,128)(2,1)S(1)}, bf16[1,256,2304]{2,1,0:T(8,128)(2,1)S(1)}, u32[]{:S(2)}, u32[]{:S(2)}) collective-permute-start(bf16[1,256,2304]{2,1,0:T(8,128)(2,1)S(1)} %dynamic-slice_convert_fusion.3), channel_id=1, source_target_pairs={{0,8},{4,12},{8,0},{12,4},{1,9},{5,13},{9,1},{13,5},{2,10},{6,14},... | collective-permute-start | bytes 3538952 | tf_op jit(solution)/shard_map/ppermute | solution.py:37
  173.8 2.7 copy-start.2
  177.9 52.1 %collective-permute-start.3 = (bf16[1,256,3072]{2,1,0:T(8,128)(2,1)}, bf16[1,256,3072]{2,1,0:T(8,128)(2,1)}, u32[]{:S(2)}, u32[]{:S(2)}) collective-permute-start(bf16[1,256,3072]{2,1,0:T(8,128)(2,1)} %dynamic-slice_convert_fusion.2), channel_id=1, source_target_pairs={{0,8},{4,12},{8,0},{12,4},{1,9},{5,13},{9,1},{13,5},{2,10},{6,14},... | collective-permute-start | bytes 4718600 | tf_op jit(solution)/shard_map/ppermute | solution.py:37
  215.7 5.3 %copy-start.7 = (f32[4,64,64]{1,2,0:T(8,128)S(1)}, f32[4,64,64]{1,2,0:T(8,128)}, u32[]{:S(2)}) copy-start(f32[4,64,64]{1,2,0:T(8,128)} %compare_convert_fusion) | copy-start | bytes 196612
  218.6 2.8 copy-start.3
  226.9 150.8 %all-gather.8.cloned.1.call-start = ((), (), s32[]{:S(2)}) async-start(), calls=%async_computation.6 | async-start | bytes 7864320 | tf_op jit(solution)/shard_map/all_gather | solution.py:97
  264.6 119.2 %all-to-all-start.2 = ((bf16[256,4,768]{2,0,1:T(8,128)(2,1)}), bf16[256,4,768]{2,0,1:T(8,128)(2,1)}, u32[]{:S(2)}, u32[]{:S(2)}) async-start(bf16[256,4,768]{2,0,1:T(8,128)(2,1)} %bitcast.142), calls=%async_computation.2 | async-start | bytes 3145728 | tf_op jit(solution)/shard_map/all_to_all | solution.py:98
  383.8 75.9 %all-to-all-start.3 = ((bf16[256,4,3072]{2,0,1:T(8,128)(2,1)}), bf16[256,4,3072]{2,0,1:T(8,128)(2,1)}, u32[]{:S(2)}, u32[]{:S(2)}) async-start(bf16[256,4,3072]{2,0,1:T(8,128)(2,1)} %bitcast.137), calls=%async_computation.3 | async-start | bytes 12582912 | tf_op jit(solution)/shard_map/all_to_all | solution.py:99
  474.6 4.5 copy-start.6
  474.6 3.5 collective-permute-start.4
  478.7 28.1 %collective-permute-start.5 = (bf16[1,256,1536]{2,1,0:T(8,128)(2,1)S(1)}, bf16[1,256,1536]{2,1,0:T(8,128)(2,1)S(1)}, u32[]{:S(2)}, u32[]{:S(2)}) collective-permute-start(bf16[1,256,1536]{2,1,0:T(8,128)(2,1)S(1)} %dynamic-slice_convert_fusion.4), channel_id=1, source_target_pairs={{0,8},{4,12},{8,0},{12,4},{1,9},{5,13},{9,1},{13,5},{2,10},{6,14},... | collective-permute-start | bytes 2359304 | tf_op jit(solution)/shard_map/ppermute | solution.py:37
Sparse Core Ops, SparseCore 0:
  9.1 66.1 all-gather.3
  227.1 34.8 all-gather.5
  263.5 114.2 all-gather.7

commit v2 on v1

v2 whole, which is shorter than its diff:
```python
import jax
import jax.numpy as jnp
from jax import lax
from jax.sharding import PartitionSpec as P

HDIM = 128
IMGS = 2
CHUNKS = 2


def layer_norm(values, eps, axes):
    mean = jnp.mean(values, axis=axes, keepdims=True)
    centred = values - mean
    variance = jnp.mean(centred * centred, axis=axes, keepdims=True)
    return centred * lax.rsqrt(variance + eps)


def attend(qkv, same):
    senders, region, _, width = qkv.shape
    heads = width // HDIM
    query_raw, key_raw, values = (
        qkv[:, :, part].reshape(senders, region, heads, HDIM) for part in range(3)
    )
    query_n = layer_norm(query_raw.astype(jnp.float32), 1e-06, -1).astype(jnp.bfloat16)
    key_n = layer_norm(key_raw.astype(jnp.float32), 1e-06, -1).astype(jnp.bfloat16)
    scores = jnp.einsum(
        "sqhd,skhd->shqk", query_n, key_n, preferred_element_type=jnp.float32
    ) * (1.0 / HDIM**0.5)
    probs = jnp.exp(scores) * same[:, None]
    weights = (probs / jnp.sum(probs, axis=-1, keepdims=True)).astype(jnp.bfloat16)
    result = jnp.einsum(
        "shqk,skhd->sqhd", weights, values, preferred_element_type=jnp.float32
    ).astype(jnp.bfloat16)
    return result.reshape(senders, region, width)


def exchange(values, n_dp, step):
    return lax.ppermute(values, "dp", [(index, index ^ step) for index in range(n_dp)])


def relative(values, me):
    count = values.shape[0]
    return [lax.dynamic_index_in_dim(values, me ^ j, 0, keepdims=False) for j in range(count)]


def product_sum(blocks, weights, n_dp):
    far = jnp.concatenate([blocks[3], blocks[1]], axis=0)
    near = jnp.concatenate([blocks[2], blocks[0]], axis=0)
    rows = blocks[0].shape[0]
    sent = jnp.dot(far, weights, preferred_element_type=jnp.float32).astype(jnp.bfloat16)
    got = exchange(sent, n_dp, 1)
    kept = jnp.dot(near, weights, preferred_element_type=jnp.float32)
    across = (kept[:rows] + got[:rows].astype(jnp.float32)).astype(jnp.bfloat16)
    across = exchange(across, n_dp, 2)
    return kept[rows:] + got[rows:].astype(jnp.float32) + across.astype(jnp.float32)


def make(n_dp, n_mp):
    assert n_dp == 4 and n_mp % n_dp == 0
    each = n_mp // n_dp

    def gather_spread(values, me):
        rows, cols = values.shape
        gathered = lax.all_gather(values, "mp", axis=0, tiled=False)
        gathered = gathered.reshape(n_dp, each, rows, cols)
        parts = relative(gathered, me)
        got = [parts[0]] + [exchange(parts[k], n_dp, k) for k in range(1, n_dp)]
        return [part.transpose(1, 0, 2).reshape(rows, each * cols) for part in got]

    def shards(tokens, counts, ln_gain, w_qkv, w_up, w_out, w_down):
        rows, cols = tokens.shape
        depth, _, part_cols = w_qkv.shape
        senders = counts.shape[0]
        region = rows // senders
        piece = region // CHUNKS
        me = lax.axis_index("dp")
        w_qkv = w_qkv.reshape(depth, 3 * part_cols)

        by_receiver = relative(tokens.reshape(senders, region, cols), me)
        own = jnp.stack(by_receiver, axis=0)
        gain = ln_gain.reshape(n_dp, each, 1, 1, cols)

        def feed(chunk):
            mine = own[:, chunk * piece : (chunk + 1) * piece].reshape(senders * piece, cols)
            gathered = lax.all_gather(mine, "mp", axis=0, tiled=False)
            gathered = gathered.reshape(n_dp, each, senders * piece, cols)
            normed = layer_norm(gathered.astype(jnp.float32), 1e-06, (0, 1, 3))
            normed = (normed * gain.reshape(n_dp, each, 1, cols)).astype(jnp.bfloat16)
            parts = relative(normed, me)
            got = [parts[0]] + [exchange(parts[k], n_dp, k) for k in range(1, n_dp)]
            got = [
                part.transpose(1, 0, 2).reshape(senders, piece, each * cols) for part in got
            ]
            return [
                jnp.concatenate([got[j ^ i][i] for i in range(senders)], axis=0)
                for j in range(n_dp)
            ]

        fed, hidden, qkv = [], [], []
        for chunk in range(CHUNKS):
            fed.append(feed(chunk))
        moved = [by_receiver[0]] + [exchange(by_receiver[i], n_dp, i) for i in range(1, senders)]
        moved = jnp.stack(moved, axis=0)

        for chunk in range(CHUNKS):
            part = product_sum(fed[chunk], w_up, n_dp)
            hidden.append(jax.nn.gelu(part, approximate=False).astype(jnp.bfloat16))
            part = product_sum(fed[chunk], w_qkv, n_dp).astype(jnp.bfloat16)
            qkv.append(part.reshape(senders, piece, 3, part_cols))

        order = jnp.arange(senders) ^ me
        theirs = lax.dynamic_index_in_dim(counts, me, axis=1, keepdims=False)[order]
        bounds = jnp.cumsum(theirs, axis=-1)
        position = jnp.arange(region)
        segment = jnp.sum((position[None, :, None] >= bounds[:, None, :]).astype(jnp.int32), axis=-1)
        same = (segment[:, :, None] == segment[:, None, :]).astype(jnp.float32)

        qkv = jnp.concatenate(qkv, axis=1)
        if part_cols % HDIM:
            everything = lax.all_gather(qkv, "mp", axis=3, tiled=True)
            attended = attend(everything, same)
            attended = lax.dynamic_slice_in_dim(
                attended, lax.axis_index("mp") * part_cols, part_cols, axis=2
            )
        else:
            attended = attend(qkv, same)

        attended, moved = lax.optimization_barrier((attended, moved))
        spread = [gather_spread(part, me) for part in hidden[:-1]]
        looked = gather_spread(attended.reshape(rows, part_cols), me)
        spread.append(gather_spread(hidden[-1], me))
        out = []
        for chunk in range(CHUNKS):
            blocks = []
            for j in range(n_dp):
                seen = looked[j].reshape(senders, region, -1)
                seen = seen[:, chunk * piece : (chunk + 1) * piece]
                blocks.append((seen.reshape(senders * piece, -1), spread[chunk][j]))
            out.append(mix(blocks, w_out, w_down, n_dp).reshape(senders, piece, cols))
        mixed = moved.astype(jnp.float32) + jnp.concatenate(out, axis=1)
        mixed = mixed.astype(jnp.bfloat16)
        return jnp.concatenate(relative(mixed, me), axis=0)

    return shards


def mix(blocks, w_out, w_down, n_dp):
    rows = blocks[0][0].shape[0]

    def product(first, second):
        seen = jnp.concatenate([blocks[first][0], blocks[second][0]], axis=0)
        units = jnp.concatenate([blocks[first][1], blocks[second][1]], axis=0)
        total = jnp.dot(seen, w_out, preferred_element_type=jnp.float32)
        return total + jnp.dot(units, w_down, preferred_element_type=jnp.float32)

    got = exchange(product(3, 1).astype(jnp.bfloat16), n_dp, 1)
    kept = product(2, 0)
    across = (kept[:rows] + got[:rows].astype(jnp.float32)).astype(jnp.bfloat16)
    across = exchange(across, n_dp, 2)
    return kept[rows:] + got[rows:].astype(jnp.float32) + across.astype(jnp.float32)


def solution(mesh):
    return jax.shard_map(
        make(mesh.shape["dp"], mesh.shape["mp"]),
        mesh=mesh,
        in_specs=(
            P(("group", "dp"), "mp"),
            P("group", None, None),
            P(),
            P("dp", None, "mp"),
            P("dp", "mp"),
            P("dp", "mp"),
            P("dp", "mp"),
        ),
        out_specs=P(("group", "dp"), "mp"),
        check_vma=False,
    )
```

time: 516 us -> 456 us (0.88); the launches traced: 515 us -> 448 us
  waiting for transfers between devices: 314 us -> 282 us
  blocking collectives: 27.7 us -> 0 us
  local copies, waits for them, and re-layouts: 53.6 us -> 35.4 us
  matrix products: 44.3 us -> 52.2 us
    ppermute x6 -> x30, waiting for transfers between devices: 24.9 us -> 154 us  [exchange(): lax.ppermute(values, 'dp', [(index, index ^ step) for index in range(n_dp)])]
    all_to_all x3 -> x0, waiting for transfers between devices: 91.4 us -> none  [the longest x1 64.8 us: shards(): lax.all_to_all(hidden, 'dp', split_axis=1, concat_axis=0, tiled=True)]
    all_gather x3 -> x5, waiting for transfers between devices: 198 us -> 127 us  [the longest x3 65.6 us: gather_spread(): gathered = lax.all_gather(values, 'mp', axis=0, tiled=False)]
    all_to_all x1 -> x0, blocking collectives: 27.7 us -> none  [shards(): lax.all_to_all(tokens, 'dp', split_axis=0, concat_axis=0, tiled=True)]
    ppermute x6 -> x30, starting transfers between devices: 2.74 us -> 21.6 us  [exchange(): lax.ppermute(values, 'dp', [(index, index ^ step) for index in range(n_dp)])]
    all_to_all x3 -> x0, starting transfers between devices: 14.2 us -> none  [the longest x1 5.24 us: shards(): lax.all_to_all(hidden, 'dp', split_axis=1, concat_axis=0, tiled=True)]
    all_to_all x3 -> x0, local copies, waits for them, and re-layouts: 13.5 us -> none  [the longest x1 6.03 us: shards(): lax.all_to_all(hidden, 'dp', split_axis=1, concat_axis=0, tiled=True)]
    unnamed x23 -> x88, local copies, waits for them, and re-layouts: 23.2 us -> 13.2 us
  transfers between devices with their start and end apart: 12 -> 35, of which waited for: 9 -> 20; matrix products, arithmetic and copies ran while one was open for 17% -> 27% of each run, Pallas kernels for 0% -> 0%
where the time goes in v2:
time: 456 us; the launch traced here: 448 us
  waiting for transfers between devices  282 us (62%)
  matrix products  52.2 us (11%)
  other arithmetic  42.7 us (9%)
  local copies, waits for them, and re-layouts  35.4 us (8%)
  starting transfers between devices  21.8 us (5%)
  between operations  14.2 us (3%)
    ppermute x30, waiting for transfers between devices, exchange(): lax.ppermute(values, 'dp', [(index, index ^ step) for index in range(n_dp)])  154 us
    all_gather x3, waiting for transfers between devices, gather_spread(): gathered = lax.all_gather(values, 'mp', axis=0, tiled=False)  65.6 us
    all_gather x2, waiting for transfers between devices, feed(): gathered = lax.all_gather(mine, 'mp', axis=0, tiled=False)  61.3 us
    ppermute x30, starting transfers between devices, exchange(): lax.ppermute(values, 'dp', [(index, index ^ step) for index in range(n_dp)])  21.6 us
    dot_general x4, matrix products, product(): return total + jnp.dot(units, w_down, preferred_element_type=jnp.float32)  14.9 us
    dot_general x4, matrix products, product_sum(): jnp.dot(far, weights, preferred_element_type=jnp.float32)  14.3 us
    dot_general x4, matrix products, product_sum(): kept = jnp.dot(near, weights, preferred_element_type=jnp.float32)  13.5 us
    unnamed x88, local copies, waits for them, and re-layouts  13.2 us
  transfers between devices with their start and end apart: 35, of which 20 were waited for; matrix products, arithmetic and copies ran while one was open for 27% of the time, Pallas kernels for 0%

profile of v2, /device:TPU:0, one launch (start us, length us, event | category | flops | bytes accessed | tf_op | source)
XLA Modules:
  0.0 448.4 jit_solution(8763711500991190621)
XLA Ops:
  6.5 1.4 constant_dynamic-slice_fusion.19
  8.5 2.6 collective-permute-start.11
  11.1 5.7 %collective-permute-done.11 = bf16[64,1536]{1,0:T(8,128)(2,1)S(1)} collective-permute-done((bf16[64,1536]{1,0:T(8,128)(2,1)S(1)}, bf16[64,1536]{1,0:T(8,128)(2,1)S(1)}, u32[]{:S(2)}, u32[]{:S(2)}) %collective-permute-start.11) | collective-permute-done | bytes 196640 | tf_op jit(solution)/shard_map/ppermute | solution.py:38
  16.8 3.7 collective-permute-done.12
  23.3 10.3 %copy.27 = bf16[1536,3,768]{0,2,1:T(8,128)(2,1)} copy(bf16[1536,3,768]{2,0,1:T(8,128)(2,1)} %param.10) | data formatting | bytes 14155776 | tf_op args[3]
  34.8 26.2 %all-gather.8.cloned.1.call-done = bf16[4,128,1536]{2,1,0:T(8,128)(2,1)} async-done(((bf16[1,128,1536]{2,1,0:T(8,128)(2,1)}), bf16[4,128,1536]{2,1,0:T(8,128)(2,1)}) %all-gather.8.cloned.1.call-update) | async-done | bytes 1572880 | tf_op jit(solution)/shard_map/all_gather | solution.py:85
  61.0 1.8 convert_reduce_fusion.1
  63.5 35.1 %all-gather.10.cloned.1.call-done = bf16[4,128,1536]{2,1,0:T(8,128)(2,1)} async-done(((bf16[1,128,1536]{2,1,0:T(8,128)(2,1)}), bf16[4,128,1536]{2,1,0:T(8,128)(2,1)}) %all-gather.10.cloned.1.call-update) | async-done | bytes 1572880 | tf_op jit(solution)/shard_map/all_gather | solution.py:85
  98.6 1.8 convert_reduce_fusion
  100.5 2.0 fusion.4
  108.4 6.8 %collective-permute-done.6 = bf16[1,128,1536]{2,1,0:T(8,128)(2,1)S(1)} collective-permute-done((bf16[1,128,1536]{2,1,0:T(8,128)(2,1)S(1)}, bf16[1,128,1536]{2,1,0:T(8,128)(2,1)S(1)}, u32[]{:S(2)}, u32[]{:S(2)}) %collective-permute-start.6) | collective-permute-done | bytes 393248 | tf_op jit(solution)/shard_map/ppermute | solution.py:38
  115.4 8.4 %collective-permute-done.5 = bf16[1,128,1536]{2,1,0:T(8,128)(2,1)S(1)} collective-permute-done((bf16[1,128,1536]{2,1,0:T(8,128)(2,1)S(1)}, bf16[1,128,1536]{2,1,0:T(8,128)(2,1)S(1)}, u32[]{:S(2)}, u32[]{:S(2)}) %collective-permute-start.5) | collective-permute-done | bytes 393248 | tf_op jit(solution)/shard_map/ppermute | solution.py:38
  124.0 2.0 convolution_convert_fusion.2
  126.2 5.9 %collective-permute-done.1 = bf16[1,128,1536]{2,1,0:T(8,128)(2,1)S(1)} collective-permute-done((bf16[1,128,1536]{2,1,0:T(8,128)(2,1)S(1)}, bf16[1,128,1536]{2,1,0:T(8,128)(2,1)S(1)}, u32[]{:S(2)}, u32[]{:S(2)}) %collective-permute-start.1) | collective-permute-done | bytes 393248 | tf_op jit(solution)/shard_map/ppermute | solution.py:38
  132.1 8.4 %collective-permute-done = bf16[1,128,1536]{2,1,0:T(8,128)(2,1)S(1)} collective-permute-done((bf16[1,128,1536]{2,1,0:T(8,128)(2,1)S(1)}, bf16[1,128,1536]{2,1,0:T(8,128)(2,1)S(1)}, u32[]{:S(2)}, u32[]{:S(2)}) %collective-permute-start) | collective-permute-done | bytes 393248 | tf_op jit(solution)/shard_map/ppermute | solution.py:38
  140.8 2.0 convolution_convert_fusion.3
  143.0 3.9 convolution_convert_fusion.1
  146.9 4.2 fusion.139
  151.6 2.0 fusion.137
  153.6 2.0 fusion.138
  155.8 1.3 collective-permute-start.9
  159.0 13.1 %collective-permute-done.9 = bf16[128,2304]{1,0:T(8,128)(2,1)S(1)} collective-permute-done((bf16[128,2304]{1,0:T(8,128)(2,1)S(1)}, bf16[128,2304]{1,0:T(8,128)(2,1)S(1)}, u32[]{:S(2)}, u32[]{:S(2)}) %collective-permute-start.9) | collective-permute-done | bytes 589856 | tf_op jit(solution)/shard_map/ppermute | solution.py:38
  174.3 9.6 %collective-permute-done.4 = bf16[128,2304]{1,0:T(8,128)(2,1)} collective-permute-done((bf16[128,2304]{1,0:T(8,128)(2,1)}, bf16[128,2304]{1,0:T(8,128)(2,1)}, u32[]{:S(2)}, u32[]{:S(2)}) %collective-permute-start.4) | collective-permute-done | bytes 589856 | tf_op jit(solution)/shard_map/ppermute | solution.py:38
  183.9 2.6 fusion.57
  186.5 2.2 reshape.270
  188.7 1.4 constant_dynamic-update-slice_fusion.1
  190.5 5.0 %fusion.67 = (f32[4,64,768]{2,1,0:T(8,128)}, f32[4,64,768]{2,1,0:T(8,128)}) fusion(bf16[4,64,3,768]{3,2,1,0:T(4,128)(2,1)S(1)} %constant_dynamic-update-slice_fusion), kind=kLoop, calls=%fused_computation.121 | loop fusion | flops 393216 | bytes 2359296 | tf_op jit(solution)/shard_map/convert_element_type | solution.py:24
  195.4 1.3 reshape.283
  198.6 1.3 multiply_reduce_fusion.1
  199.9 2.2 reshape.284
  202.1 2.2 reduce_sum.96
  205.4 1.9 multiply_reduce_fusion
  207.4 1.3 multiply_convert_fusion
  210.0 3.1 slice_reduce_fusion
  213.2 1.3 fusion.51
  215.4 1.9 fusion.20
  217.3 1.4 collective-permute-start.15
  218.7 17.4 %collective-permute-done.15 = bf16[128,3072]{1,0:T(8,128)(2,1)S(1)} collective-permute-done((bf16[128,3072]{1,0:T(8,128)(2,1)S(1)}, bf16[128,3072]{1,0:T(8,128)(2,1)S(1)}, u32[]{:S(2)}, u32[]{:S(2)}) %collective-permute-start.15) | collective-permute-done | bytes 786464 | tf_op jit(solution)/shard_map/ppermute | solution.py:38
  236.1 5.8 %fusion.14 = bf16[128,3072]{1,0:T(8,128)(2,1)} fusion(bf16[128,3072]{1,0:T(8,128)(2,1)S(1)} %collective-permute-done.15, f32[256,3072]{1,0:T(8,128)S(1)} %copy-done.7, bf16[256,3072]{1,0:T(8,128)(2,1)} %collective-permute-done.14), kind=kLoop, calls=%fused_computation.29 | loop fusion | flops 27131904 | bytes 3932160 | tf_op jit(solution)/shard_map/convert_element_type | solution.py:107
  242.0 6.4 %convolution_convert_fusion = bf16[256,3072]{1,0:T(8,128)(2,1)S(1)} fusion(bf16[256,1536]{1,0:T(8,128)(2,1)S(1)} %copy-done.20, bf16[1536,3072]{1,0:T(8,128)(2,1)} %param.11), kind=kOutput, calls=%fused_computation.5 | convolution fusion | flops 2416705536 | bytes 11796480 | tf_op jit(solution)/shard_map/dot_general | solution.py:50
  248.4 5.2 %fusion.140 = f32[256,3072]{1,0:T(8,128)S(1)} fusion(bf16[256,1536]{1,0:T(8,128)(2,1)S(1)} %copy-done.22, bf16[1536,3072]{1,0:T(8,128)(2,1)} %param.11), kind=kOutput, calls=%fused_computation.273 | convolution fusion | flops 2415919104 | bytes 13369344 | tf_op jit(solution)/shard_map/dot_general | solution.py:52
  253.8 1.4 collective-permute-start.24
  255.2 18.6 %collective-permute-done.24 = bf16[128,3072]{1,0:T(8,128)(2,1)S(1)} collective-permute-done((bf16[128,3072]{1,0:T(8,128)(2,1)S(1)}, bf16[128,3072]{1,0:T(8,128)(2,1)S(1)}, u32[]{:S(2)}, u32[]{:S(2)}) %collective-permute-start.24) | collective-permute-done | bytes 786464 | tf_op jit(solution)/shard_map/ppermute | solution.py:38
  273.8 4.4 fusion.17
  278.3 1.5 constant_dynamic-slice_fusion.6
  282.0 9.2 %collective-permute-done.17 = bf16[1,256,768]{2,1,0:T(8,128)(2,1)S(1)} collective-permute-done((bf16[1,256,768]{2,1,0:T(8,128)(2,1)S(1)}, bf16[1,256,768]{2,1,0:T(8,128)(2,1)S(1)}, u32[]{:S(2)}, u32[]{:S(2)}) %collective-permute-start.17) | collective-permute-done | bytes 393248 | tf_op jit(solution)/shard_map/ppermute | solution.py:38
  291.3 8.3 %collective-permute-done.13 = bf16[1,256,768]{2,1,0:T(8,128)(2,1)S(1)} collective-permute-done((bf16[1,256,768]{2,1,0:T(8,128)(2,1)S(1)}, bf16[1,256,768]{2,1,0:T(8,128)(2,1)S(1)}, u32[]{:S(2)}, u32[]{:S(2)}) %collective-permute-start.13) | collective-permute-done | bytes 393248 | tf_op jit(solution)/shard_map/ppermute | solution.py:38
  299.7 2.0 fusion.74
  301.6 2.0 fusion.70
  303.6 11.6 %all-gather.14.cloned.1.call-done = bf16[512,3072]{1,0:T(8,128)(2,1)} async-done(((bf16[128,3072]{1,0:T(8,128)(2,1)}), bf16[512,3072]{1,0:T(8,128)(2,1)}) %all-gather.14.cloned.1.call-update) | async-done | bytes 3145744 | tf_op jit(solution)/shard_map/all_gather | solution.py:64
  315.3 3.6 constant_dynamic-slice_fusion.4
  320.5 2.0 fusion.82
  322.4 2.0 fusion.78
  324.9 53.9 %all-gather.16.cloned.1.call-done = bf16[512,3072]{1,0:T(8,128)(2,1)} async-done(((bf16[128,3072]{1,0:T(8,128)(2,1)}), bf16[512,3072]{1,0:T(8,128)(2,1)}) %all-gather.16.cloned.1.call-update) | async-done | bytes 3145744 | tf_op jit(solution)/shard_map/all_gather | solution.py:64
  378.9 2.3 constant_dynamic-slice_fusion.1
  383.4 6.9 %fusion.10 = bf16[256,1536]{1,0:T(8,128)(2,1)S(1)} fusion(f32[256,1536]{1,0:T(8,128)S(1)} %copy-done.12, bf16[3072,1536]{1,0:T(8,128)(2,1)} %param.13, bf16[128,3072]{1,0:T(8,128)(2,1)} %bitcast.60, bf16[128,3072]{1,0:T(8,128)(2,1)} %bitcast.59), kind=kOutput, calls=%fused_computation.23 | convolution fusion | flops 2419851264 | bytes 13369344 | tf_op jit(solution)/shard_map/dot_general | solution.py:154
  390.4 10.6 %collective-permute-done.26 = bf16[1,128,3072]{2,1,0:T(8,128)(2,1)S(1)} collective-permute-done((bf16[1,128,3072]{2,1,0:T(8,128)(2,1)S(1)}, bf16[1,128,3072]{2,1,0:T(8,128)(2,1)S(1)}, u32[]{:S(2)}, u32[]{:S(2)}) %collective-permute-start.26) | collective-permute-done | bytes 786464 | tf_op jit(solution)/shard_map/ppermute | solution.py:38
  401.1 2.6 fusion.11
  403.9 2.6 convolution_add_fusion.3
  406.6 11.3 %collective-permute-done.25 = bf16[1,128,3072]{2,1,0:T(8,128)(2,1)S(1)} collective-permute-done((bf16[1,128,3072]{2,1,0:T(8,128)(2,1)S(1)}, bf16[1,128,3072]{2,1,0:T(8,128)(2,1)S(1)}, u32[]{:S(2)}, u32[]{:S(2)}) %collective-permute-start.25) | collective-permute-done | bytes 786464 | tf_op jit(solution)/shard_map/ppermute | solution.py:38
  417.9 2.7 convolution_add_fusion.1
  420.7 1.5 collective-permute-start.22
  423.0 9.8 %collective-permute-done.22 = bf16[128,1536]{1,0:T(8,128)(2,1)S(1)} collective-permute-done((bf16[128,1536]{1,0:T(8,128)(2,1)S(1)}, bf16[128,1536]{1,0:T(8,128)(2,1)S(1)}, u32[]{:S(2)}, u32[]{:S(2)}) %collective-permute-start.22) | collective-permute-done | bytes 393248 | tf_op jit(solution)/shard_map/ppermute | solution.py:38
  432.9 7.4 %collective-permute-done.29 = bf16[128,1536]{1,0:T(8,128)(2,1)S(1)} collective-permute-done((bf16[128,1536]{1,0:T(8,128)(2,1)S(1)}, bf16[128,1536]{1,0:T(8,128)(2,1)S(1)}, u32[]{:S(2)}, u32[]{:S(2)}) %collective-permute-start.29) | collective-permute-done | bytes 393248 | tf_op jit(solution)/shard_map/ppermute | solution.py:38
  (188 shorter events, 31.7 us)
Async XLA Ops:
  6.5 293.1 %copy-start = (bf16[768,1536]{1,0:T(8,128)(2,1)S(1)}, bf16[768,1536]{1,0:T(8,128)(2,1)}, u32[]{:S(2)}) copy-start(bf16[768,1536]{1,0:T(8,128)(2,1)} %param.12) | copy-start | bytes 7077892
  6.5 54.5 %all-gather.8.cloned.1.call-start = ((), (), s32[]{:S(2)}) async-start(), calls=%async_computation | async-start | bytes 1966080 | tf_op jit(solution)/shard_map/all_gather | solution.py:85
  8.0 3.2 collective-permute-start.10
  8.5 8.3 %collective-permute-start.11 = (bf16[64,1536]{1,0:T(8,128)(2,1)S(1)}, bf16[64,1536]{1,0:T(8,128)(2,1)S(1)}, u32[]{:S(2)}, u32[]{:S(2)}) collective-permute-start(bf16[64,1536]{1,0:T(8,128)(2,1)S(1)} %bitcast.242), channel_id=1, source_target_pairs={{0,8},{4,12},{8,0},{12,4},{1,9},{5,13},{9,1},{13,5},{2,10},{6,14},... | collective-permute-start | bytes 589832 | tf_op jit(solution)/shard_map/ppermute | solution.py:38
  11.0 9.4 %collective-permute-start.12 = (bf16[64,1536]{1,0:T(8,128)(2,1)S(1)}, bf16[64,1536]{1,0:T(8,128)(2,1)S(1)}, u32[]{:S(2)}, u32[]{:S(2)}) collective-permute-start(bf16[64,1536]{1,0:T(8,128)(2,1)S(1)} %bitcast.241), channel_id=1, source_target_pairs={{0,12},{4,8},{8,4},{12,0},{1,13},{5,9},{9,5},{13,1},{2,14},{6,10},... | collective-permute-start | bytes 589832 | tf_op jit(solution)/shard_map/ppermute | solution.py:38
  22.5 76.1 %all-gather.10.cloned.1.call-start = ((), (), s32[]{:S(2)}) async-start(), calls=%async_computation.1 | async-start | bytes 1966080 | tf_op jit(solution)/shard_map/all_gather | solution.py:85
  23.2 255.1 %all-gather.12.cloned.1.call-start = ((), (), s32[]{:S(2)}) async-start(), calls=%async_computation.2 | async-start | bytes 1966080 | tf_op jit(solution)/shard_map/all_gather | solution.py:64
  23.3 10.3 %copy-start.23 = (s32[4,4,2]{1,2,0:T(2,128)S(1)}, s32[4,4,2]{1,2,0:T(2,128)}, u32[]{:S(2)}) copy-start(s32[4,4,2]{1,2,0:T(2,128)} %param.8) | copy-start | bytes 388
  61.0 1.9 copy-start.2
  98.6 3.8 copy-start.3
  98.6 3.9 copy-start.4
  102.5 21.5 %slice-start = ((s8[7077888]{0:T(1024)(128)(4,1)}), s8[4194304]{0:T(1024)(128)(4,1)S(1)}, s32[]{:S(2)}) async-start(s8[7077888]{0:T(1024)(128)(4,1)} %bitcast.218), calls=%async_computation.5 | async-start | bytes 8388608
  103.7 20.3 %slice-start.1 = ((s8[7077888]{0:T(1024)(128)(4,1)}), s8[2883584]{0:T(1024)(128)(4,1)S(1)}, s32[]{:S(2)}) async-start(s8[7077888]{0:T(1024)(128)(4,1)} %bitcast.218), calls=%async_computation.6 | async-start | bytes 5767168
  103.8 11.5 %collective-permute-start.6 = (bf16[1,128,1536]{2,1,0:T(8,128)(2,1)S(1)}, bf16[1,128,1536]{2,1,0:T(8,128)(2,1)S(1)}, u32[]{:S(2)}, u32[]{:S(2)}) collective-permute-start(bf16[1,128,1536]{2,1,0:T(8,128)(2,1)S(1)} %get-tuple-element.25), channel_id=1, source_target_pairs={{0,12},{4,8},{8,4},{12,0},{1,13},{5,9},{9,5},{13,1},{2,14},{6,10},... | collective-permute-start | bytes 1179656 | tf_op jit(solution)/shard_map/ppermute | solution.py:38
  105.4 18.3 %collective-permute-start.5 = (bf16[1,128,1536]{2,1,0:T(8,128)(2,1)S(1)}, bf16[1,128,1536]{2,1,0:T(8,128)(2,1)S(1)}, u32[]{:S(2)}, u32[]{:S(2)}) collective-permute-start(bf16[1,128,1536]{2,1,0:T(8,128)(2,1)S(1)} %get-tuple-element.26), channel_id=1, source_target_pairs={{0,8},{4,12},{8,0},{12,4},{1,9},{5,13},{9,1},{13,5},{2,10},{6,14},... | collective-permute-start | bytes 1179656 | tf_op jit(solution)/shard_map/ppermute | solution.py:38
  106.1 17.6 %collective-permute-start.7 = (bf16[1,128,1536]{2,1,0:T(8,128)(2,1)S(1)}, bf16[1,128,1536]{2,1,0:T(8,128)(2,1)S(1)}, u32[]{:S(2)}, u32[]{:S(2)}) collective-permute-start(bf16[1,128,1536]{2,1,0:T(8,128)(2,1)S(1)} %get-tuple-element.23), channel_id=1, source_target_pairs={{0,4},{4,0},{8,12},{12,8},{1,5},{5,1},{9,13},{13,9},{2,6},{6,2},{1... | collective-permute-start | bytes 1179656 | tf_op jit(solution)/shard_map/ppermute | solution.py:38
  106.6 25.5 %collective-permute-start.1 = (bf16[1,128,1536]{2,1,0:T(8,128)(2,1)S(1)}, bf16[1,128,1536]{2,1,0:T(8,128)(2,1)S(1)}, u32[]{:S(2)}, u32[]{:S(2)}) collective-permute-start(bf16[1,128,1536]{2,1,0:T(8,128)(2,1)S(1)} %get-tuple-element.29), channel_id=1, source_target_pairs={{0,12},{4,8},{8,4},{12,0},{1,13},{5,9},{9,5},{13,1},{2,14},{6,10},... | collective-permute-start | bytes 1179656 | tf_op jit(solution)/shard_map/ppermute | solution.py:38
  107.7 32.8 %collective-permute-start = (bf16[1,128,1536]{2,1,0:T(8,128)(2,1)S(1)}, bf16[1,128,1536]{2,1,0:T(8,128)(2,1)S(1)}, u32[]{:S(2)}, u32[]{:S(2)}) collective-permute-start(bf16[1,128,1536]{2,1,0:T(8,128)(2,1)S(1)} %get-tuple-element.30), channel_id=1, source_target_pairs={{0,8},{4,12},{8,0},{12,4},{1,9},{5,13},{9,1},{13,5},{2,10},{6,14},... | collective-permute-start | bytes 1179656 | tf_op jit(solution)/shard_map/ppermute | solution.py:38
  115.2 25.3 %collective-permute-start.2 = (bf16[1,128,1536]{2,1,0:T(8,128)(2,1)S(1)}, bf16[1,128,1536]{2,1,0:T(8,128)(2,1)S(1)}, u32[]{:S(2)}, u32[]{:S(2)}) collective-permute-start(bf16[1,128,1536]{2,1,0:T(8,128)(2,1)S(1)} %get-tuple-element.27), channel_id=1, source_target_pairs={{0,4},{4,0},{8,12},{12,8},{1,5},{5,1},{9,13},{13,9},{2,6},{6,2},{1... | collective-permute-start | bytes 1179656 | tf_op jit(solution)/shard_map/ppermute | solution.py:38
  123.9 2.1 copy-start.19
  124.0 19.0 %slice-start.2 = ((s8[9437184]{0:T(1024)(128)(4,1)}), s8[4194304]{0:T(1024)(128)(4,1)S(1)}, s32[]{:S(2)}) async-start(s8[9437184]{0:T(1024)(128)(4,1)} %bitcast.251), calls=%async_computation.7 | async-start | bytes 8388608
  124.0 19.0 %slice-start.3 = ((s8[9437184]{0:T(1024)(128)(4,1)}), s8[4194304]{0:T(1024)(128)(4,1)S(1)}, s32[]{:S(2)}) async-start(s8[9437184]{0:T(1024)(128)(4,1)} %bitcast.251), calls=%async_computation.8 | async-start | bytes 8388608
  126.0 29.6 %collective-permute-start.8 = (bf16[256,2304]{1,0:T(8,128)(2,1)S(1)}, bf16[256,2304]{1,0:T(8,128)(2,1)S(1)}, u32[]{:S(2)}, u32[]{:S(2)}) collective-permute-start(bf16[256,2304]{1,0:T(8,128)(2,1)S(1)} %convolution_convert_fusion.2), channel_id=1, source_target_pairs={{0,4},{4,0},{8,12},{12,8},{1,5},{5,1},{9,13},{13,9},{2,6},{6,2},{1... | collective-permute-start | bytes 3538952 | tf_op jit(solution)/shard_map/ppermute | solution.py:38
  140.8 2.2 slice-start.4
  142.8 14.3 %collective-permute-start.3 = (bf16[256,2304]{1,0:T(8,128)(2,1)S(1)}, bf16[256,2304]{1,0:T(8,128)(2,1)S(1)}, u32[]{:S(2)}, u32[]{:S(2)}) collective-permute-start(bf16[256,2304]{1,0:T(8,128)(2,1)S(1)} %convolution_convert_fusion.3), channel_id=1, source_target_pairs={{0,4},{4,0},{8,12},{12,8},{1,5},{5,1},{9,13},{13,9},{2,6},{6,2},{1... | collective-permute-start | bytes 3538952 | tf_op jit(solution)/shard_map/ppermute | solution.py:38
  151.1 64.3 %collective-permute-start.14 = (bf16[256,3072]{1,0:T(8,128)(2,1)}, bf16[256,3072]{1,0:T(8,128)(2,1)}, u32[]{:S(2)}, u32[]{:S(2)}) collective-permute-start(bf16[256,3072]{1,0:T(8,128)(2,1)} %convolution_convert_fusion.1), channel_id=1, source_target_pairs={{0,4},{4,0},{8,12},{12,8},{1,5},{5,1},{9,13},{13,9},{2,6},{6,2},{1... | collective-permute-start | bytes 4718600 | tf_op jit(solution)/shard_map/ppermute | solution.py:38
  151.6 2.0 copy-start.21
  153.6 3.5 copy-start.9
  155.8 16.2 %collective-permute-start.9 = (bf16[128,2304]{1,0:T(8,128)(2,1)S(1)}, bf16[128,2304]{1,0:T(8,128)(2,1)S(1)}, u32[]{:S(2)}, u32[]{:S(2)}) collective-permute-start(bf16[128,2304]{1,0:T(8,128)(2,1)S(1)} %fusion.52), channel_id=1, source_target_pairs={{0,8},{4,12},{8,0},{12,4},{1,9},{5,13},{9,1},{13,5},{2,10},{6,14},... | collective-permute-start | bytes 1769480 | tf_op jit(solution)/shard_map/ppermute | solution.py:38
  157.1 14.9 %copy-start.14 = (bf16[256,2304]{1,0:T(8,128)(2,1)}, bf16[256,2304]{1,0:T(8,128)(2,1)S(1)}, u32[]{:S(2)}) copy-start(bf16[256,2304]{1,0:T(8,128)(2,1)S(1)} %collective-permute-done.3) | copy-start | bytes 3538948
  158.2 25.7 %collective-permute-start.4 = (bf16[128,2304]{1,0:T(8,128)(2,1)}, bf16[128,2304]{1,0:T(8,128)(2,1)}, u32[]{:S(2)}, u32[]{:S(2)}) collective-permute-start(bf16[128,2304]{1,0:T(8,128)(2,1)} %fusion.55), channel_id=1, source_target_pairs={{0,8},{4,12},{8,0},{12,4},{1,9},{5,13},{9,1},{13,5},{2,10},{6,14},... | collective-permute-start | bytes 1769480 | tf_op jit(solution)/shard_map/ppermute | solution.py:38
  190.5 5.0 %copy-start.5 = (bf16[4,64,3,768]{3,2,1,0:T(4,128)(2,1)}, bf16[4,64,3,768]{3,2,1,0:T(4,128)(2,1)S(1)}, u32[]{:S(2)}) copy-start(bf16[4,64,3,768]{3,2,1,0:T(4,128)(2,1)S(1)} %constant_dynamic-update-slice_fusion) | copy-start | bytes 3538948
  204.4 2.9 copy-start.16
  204.4 3.0 copy-start.1
  215.3 99.9 %all-gather.14.cloned.1.call-start = ((), (), s32[]{:S(2)}) async-start(), calls=%async_computation.3 | async-start | bytes 3932160 | tf_op jit(solution)/shard_map/all_gather | solution.py:64
  215.4 20.7 %copy-start.7 = (f32[256,3072]{1,0:T(8,128)S(1)}, f32[256,3072]{1,0:T(8,128)}, u32[]{:S(2)}) copy-start(f32[256,3072]{1,0:T(8,128)} %fusion.139) | copy-start | bytes 9437188
  217.3 24.6 %copy-start.20 = (bf16[256,1536]{1,0:T(8,128)(2,1)S(1)}, bf16[256,1536]{1,0:T(8,128)(2,1)}, u32[]{:S(2)}) copy-start(bf16[256,1536]{1,0:T(8,128)(2,1)} %copy-done.19) | copy-start | bytes 2359300
  217.3 18.8 %collective-permute-start.15 = (bf16[128,3072]{1,0:T(8,128)(2,1)S(1)}, bf16[128,3072]{1,0:T(8,128)(2,1)S(1)}, u32[]{:S(2)}, u32[]{:S(2)}) collective-permute-start(bf16[128,3072]{1,0:T(8,128)(2,1)S(1)} %fusion.20), channel_id=1, source_target_pairs={{0,8},{4,12},{8,0},{12,4},{1,9},{5,13},{9,1},{13,5},{2,10},{6,14},... | collective-permute-start | bytes 2359304 | tf_op jit(solution)/shard_map/ppermute | solution.py:38
  241.9 137.0 %all-gather.16.cloned.1.call-start = ((), (), s32[]{:S(2)}) async-start(), calls=%async_computation.4 | async-start | bytes 3932160 | tf_op jit(solution)/shard_map/all_gather | solution.py:64
  241.9 6.5 %copy-start.22 = (bf16[256,1536]{1,0:T(8,128)(2,1)S(1)}, bf16[256,1536]{1,0:T(8,128)(2,1)}, u32[]{:S(2)}) copy-start(bf16[256,1536]{1,0:T(8,128)(2,1)} %copy-done.21) | copy-start | bytes 2359300
  248.3 5.3 %collective-permute-start.23 = (bf16[256,3072]{1,0:T(8,128)(2,1)S(1)}, bf16[256,3072]{1,0:T(8,128)(2,1)S(1)}, u32[]{:S(2)}, u32[]{:S(2)}) collective-permute-start(bf16[256,3072]{1,0:T(8,128)(2,1)S(1)} %convolution_convert_fusion), channel_id=1, source_target_pairs={{0,4},{4,0},{8,12},{12,8},{1,5},{5,1},{9,13},{13,9},{2,6},{6,2},{1... | collective-permute-start | bytes 4718600 | tf_op jit(solution)/shard_map/ppermute | solution.py:38
  253.8 20.0 %collective-permute-start.24 = (bf16[128,3072]{1,0:T(8,128)(2,1)S(1)}, bf16[128,3072]{1,0:T(8,128)(2,1)S(1)}, u32[]{:S(2)}, u32[]{:S(2)}) collective-permute-start(bf16[128,3072]{1,0:T(8,128)(2,1)S(1)} %fusion.18), channel_id=1, source_target_pairs={{0,8},{4,12},{8,0},{12,4},{1,9},{5,13},{9,1},{13,5},{2,10},{6,14},... | collective-permute-start | bytes 2359304 | tf_op jit(solution)/shard_map/ppermute | solution.py:38
  279.8 11.5 %collective-permute-start.17 = (bf16[1,256,768]{2,1,0:T(8,128)(2,1)S(1)}, bf16[1,256,768]{2,1,0:T(8,128)(2,1)S(1)}, u32[]{:S(2)}, u32[]{:S(2)}) collective-permute-start(bf16[1,256,768]{2,1,0:T(8,128)(2,1)S(1)} %get-tuple-element.19), channel_id=1, source_target_pairs={{0,12},{4,8},{8,4},{12,0},{1,13},{5,9},{9,5},{13,1},{2,14},{6,10},... | collective-permute-start | bytes 1179656 | tf_op jit(solution)/shard_map/ppermute | solution.py:38
  280.6 10.7 %collective-permute-start.18 = (bf16[1,256,768]{2,1,0:T(8,128)(2,1)S(1)}, bf16[1,256,768]{2,1,0:T(8,128)(2,1)S(1)}, u32[]{:S(2)}, u32[]{:S(2)}) collective-permute-start(bf16[1,256,768]{2,1,0:T(8,128)(2,1)S(1)} %get-tuple-element.20), channel_id=1, source_target_pairs={{0,4},{4,0},{8,12},{12,8},{1,5},{5,1},{9,13},{13,9},{2,6},{6,2},{1... | collective-permute-start | bytes 1179656 | tf_op jit(solution)/shard_map/ppermute | solution.py:38
  281.3 18.3 %collective-permute-start.13 = (bf16[1,256,768]{2,1,0:T(8,128)(2,1)S(1)}, bf16[1,256,768]{2,1,0:T(8,128)(2,1)S(1)}, u32[]{:S(2)}, u32[]{:S(2)}) collective-permute-start(bf16[1,256,768]{2,1,0:T(8,128)(2,1)S(1)} %get-tuple-element.22), channel_id=1, source_target_pairs={{0,8},{4,12},{8,0},{12,4},{1,9},{5,13},{9,1},{13,5},{2,10},{6,14},... | collective-permute-start | bytes 1179656 | tf_op jit(solution)/shard_map/ppermute | solution.py:38
  318.9 64.0 %collective-permute-start.19 = (bf16[1,128,3072]{2,1,0:T(8,128)(2,1)}, bf16[1,128,3072]{2,1,0:T(8,128)(2,1)}, u32[]{:S(2)}, u32[]{:S(2)}) collective-permute-start(bf16[1,128,3072]{2,1,0:T(8,128)(2,1)} %get-tuple-element.11), channel_id=1, source_target_pairs={{0,12},{4,8},{8,4},{12,0},{1,13},{5,9},{9,5},{13,1},{2,14},{6,10},... | collective-permute-start | bytes 2359304 | tf_op jit(solution)/shard_map/ppermute | solution.py:38
  319.7 63.6 %collective-permute-start.20 = (bf16[1,128,3072]{2,1,0:T(8,128)(2,1)}, bf16[1,128,3072]{2,1,0:T(8,128)(2,1)}, u32[]{:S(2)}, u32[]{:S(2)}) collective-permute-start(bf16[1,128,3072]{2,1,0:T(8,128)(2,1)} %get-tuple-element.12), channel_id=1, source_target_pairs={{0,4},{4,0},{8,12},{12,8},{1,5},{5,1},{9,13},{13,9},{2,6},{6,2},{1... | collective-permute-start | bytes 2359304 | tf_op jit(solution)/shard_map/ppermute | solution.py:38
  324.4 79.5 %collective-permute-start.16 = (bf16[1,128,3072]{2,1,0:T(8,128)(2,1)}, bf16[1,128,3072]{2,1,0:T(8,128)(2,1)S(1)}, u32[]{:S(2)}, u32[]{:S(2)}) collective-permute-start(bf16[1,128,3072]{2,1,0:T(8,128)(2,1)} %get-tuple-element.14), channel_id=1, source_target_pairs={{0,8},{4,12},{8,0},{12,4},{1,9},{5,13},{9,1},{13,5},{2,10},{6,14},... | collective-permute-start | bytes 2359304 | tf_op jit(solution)/shard_map/ppermute | solution.py:38
  378.9 4.5 %copy-start.12 = (f32[256,1536]{1,0:T(8,128)S(1)}, f32[256,1536]{1,0:T(8,128)}, u32[]{:S(2)}) copy-start(f32[256,1536]{1,0:T(8,128)} %fusion.74) | copy-start | bytes 4718596
  378.9 22.2 %slice-start.5 = ((s8[9437184]{0:T(1024)(128)(4,1)}), s8[4194304]{0:T(1024)(128)(4,1)S(1)}, s32[]{:S(2)}) async-start(s8[9437184]{0:T(1024)(128)(4,1)} %bitcast.253), calls=%async_computation.10 | async-start | bytes 8388608
  381.2 19.9 %collective-permute-start.26 = (bf16[1,128,3072]{2,1,0:T(8,128)(2,1)S(1)}, bf16[1,128,3072]{2,1,0:T(8,128)(2,1)S(1)}, u32[]{:S(2)}, u32[]{:S(2)}) collective-permute-start(bf16[1,128,3072]{2,1,0:T(8,128)(2,1)S(1)} %get-tuple-element.15), channel_id=1, source_target_pairs={{0,12},{4,8},{8,4},{12,0},{1,13},{5,9},{9,5},{13,1},{2,14},{6,10},... | collective-permute-start | bytes 2359304 | tf_op jit(solution)/shard_map/ppermute | solution.py:38
  382.1 18.9 %collective-permute-start.27 = (bf16[1,128,3072]{2,1,0:T(8,128)(2,1)S(1)}, bf16[1,128,3072]{2,1,0:T(8,128)(2,1)S(1)}, u32[]{:S(2)}, u32[]{:S(2)}) collective-permute-start(bf16[1,128,3072]{2,1,0:T(8,128)(2,1)S(1)} %get-tuple-element.16), channel_id=1, source_target_pairs={{0,4},{4,0},{8,12},{12,8},{1,5},{5,1},{9,13},{13,9},{2,6},{6,2},{1... | collective-permute-start | bytes 2359304 | tf_op jit(solution)/shard_map/ppermute | solution.py:38
  382.8 35.1 %collective-permute-start.25 = (bf16[1,128,3072]{2,1,0:T(8,128)(2,1)S(1)}, bf16[1,128,3072]{2,1,0:T(8,128)(2,1)S(1)}, u32[]{:S(2)}, u32[]{:S(2)}) collective-permute-start(bf16[1,128,3072]{2,1,0:T(8,128)(2,1)S(1)} %get-tuple-element.18), channel_id=1, source_target_pairs={{0,8},{4,12},{8,0},{12,4},{1,9},{5,13},{9,1},{13,5},{2,10},{6,14},... | collective-permute-start | bytes 2359304 | tf_op jit(solution)/shard_map/ppermute | solution.py:38
  383.4 17.7 %copy-start.13 = (f32[256,1536]{1,0:T(8,128)S(1)}, f32[256,1536]{1,0:T(8,128)}, u32[]{:S(2)}) copy-start(f32[256,1536]{1,0:T(8,128)} %fusion.82) | copy-start | bytes 4718596
  383.4 17.7 %slice-start.6 = ((s8[9437184]{0:T(1024)(128)(4,1)}), s8[4194304]{0:T(1024)(128)(4,1)S(1)}, s32[]{:S(2)}) async-start(s8[9437184]{0:T(1024)(128)(4,1)} %bitcast.253), calls=%async_computation.11 | async-start | bytes 8388608
  383.4 17.7 %slice-start.7 = ((s8[9437184]{0:T(1024)(128)(4,1)}), s8[1048576]{0:T(1024)(128)(4,1)S(1)}, s32[]{:S(2)}) async-start(s8[9437184]{0:T(1024)(128)(4,1)} %bitcast.253), calls=%async_computation.12 | async-start | bytes 2097152
  390.3 30.3 %collective-permute-start.21 = (bf16[256,1536]{1,0:T(8,128)(2,1)S(1)}, bf16[256,1536]{1,0:T(8,128)(2,1)S(1)}, u32[]{:S(2)}, u32[]{:S(2)}) collective-permute-start(bf16[256,1536]{1,0:T(8,128)(2,1)S(1)} %fusion.10), channel_id=1, source_target_pairs={{0,4},{4,0},{8,12},{12,8},{1,5},{5,1},{9,13},{13,9},{2,6},{6,2},{1... | collective-permute-start | bytes 2359304 | tf_op jit(solution)/shard_map/ppermute | solution.py:38
  401.1 2.8 copy-start.10
  401.1 2.8 copy-start.15
  403.7 18.5 %collective-permute-start.28 = (bf16[256,1536]{1,0:T(8,128)(2,1)S(1)}, bf16[256,1536]{1,0:T(8,128)(2,1)S(1)}, u32[]{:S(2)}, u32[]{:S(2)}) collective-permute-start(bf16[256,1536]{1,0:T(8,128)(2,1)S(1)} %fusion.11), channel_id=1, source_target_pairs={{0,4},{4,0},{8,12},{12,8},{1,5},{5,1},{9,13},{13,9},{2,6},{6,2},{1... | collective-permute-start | bytes 2359304 | tf_op jit(solution)/shard_map/ppermute | solution.py:38
  403.9 14.0 %copy-start.11 = (f32[256,1536]{1,0:T(8,128)S(1)}, f32[256,1536]{1,0:T(8,128)}, u32[]{:S(2)}) copy-start(f32[256,1536]{1,0:T(8,128)} %fusion.78) | copy-start | bytes 4718596
  420.7 12.0 %collective-permute-start.22 = (bf16[128,1536]{1,0:T(8,128)(2,1)S(1)}, bf16[128,1536]{1,0:T(8,128)(2,1)S(1)}, u32[]{:S(2)}, u32[]{:S(2)}) collective-permute-start(bf16[128,1536]{1,0:T(8,128)(2,1)S(1)} %fusion.64), channel_id=1, source_target_pairs={{0,8},{4,12},{8,0},{12,4},{1,9},{5,13},{9,1},{13,5},{2,10},{6,14},... | collective-permute-start | bytes 1179656 | tf_op jit(solution)/shard_map/ppermute | solution.py:38
  422.3 18.0 %collective-permute-start.29 = (bf16[128,1536]{1,0:T(8,128)(2,1)S(1)}, bf16[128,1536]{1,0:T(8,128)(2,1)S(1)}, u32[]{:S(2)}, u32[]{:S(2)}) collective-permute-start(bf16[128,1536]{1,0:T(8,128)(2,1)S(1)} %fusion.62), channel_id=1, source_target_pairs={{0,8},{4,12},{8,0},{12,4},{1,9},{5,13},{9,1},{13,5},{2,10},{6,14},... | collective-permute-start | bytes 1179656 | tf_op jit(solution)/shard_map/ppermute | solution.py:38
  432.9 7.6 %copy-start.8 = (bf16[4,64,1536]{2,1,0:T(8,128)(2,1)S(1)}, bf16[4,64,1536]{2,1,0:T(8,128)(2,1)}, u32[]{:S(2)}) copy-start(bf16[4,64,1536]{2,1,0:T(8,128)(2,1)} %get-tuple-element.7) | copy-start | bytes 2359300
  (3 other events, 4.4 us)
Sparse Core Ops, SparseCore 0:
  22.6 38.4 all-gather.7
  62.6 35.9 all-gather.9
  215.5 35.9 all-gather.11
  252.9 62.3 all-gather.13
  316.7 62.1 all-gather.15
